TPU v7x, 32 devices: a whole 2x2x4 slice. The times are simulated.
32 devices in a mesh: sub: 8 (over z, x), slab: 4 (over y, core).
Axes of the slice: x: 2, y: 2, z: 4, core: 2. Of those that a mesh axis runs over, the one named last changes fastest.
Arguments:
- adjoint_load: float32 [4, 8, 2, 4, 3200], P('slab', 'sub')
- design: float32 [4, 8, 2032], P('slab', 'sub'), may hold values from 0 to 1
- viscous_block: float32 [24, 24], replicated
- brinkman_block: float32 [24, 24], replicated
- coupling: float32 [8, 24], replicated, may hold values from -1.2 to 1.2
- stabilization: float32 [8, 8], replicated
- neighbours: int32 [4, 8, 3], P('slab', 'sub'), may hold values from -1 to 7, as said below
- iface_nodes: int32 [4, 8, 3, 256], P('slab', 'sub'), may hold values from 0 to 3199, as said below
- iface_count: int32 [4, 8, 3], P('slab', 'sub'), may hold values from 0 to 256, as said below
- face_nodes: int32 [4, 8, 2, 512], P('slab', 'sub'), may hold values from 0 to 3199, as said below
- owner_ids: int32 [4, 8, 3, 256], P('slab', 'sub'), may hold values from 0 to 7, as said below
Outputs:
- solution: float32 [4, 8, 2, 4, 3200], P('slab', 'sub')
- coefficients: float32 [2, 3], replicated
Inputs may be any that keep to these rules, and one draw needn't show every extreme that they name: In round r the neighbour of subdomain i is i XOR 2^r or -1 for none; two neighbours list each other. `iface_nodes`: per subdomain, all entries here and in face_nodes are distinct local nodes. Slot k of round r names the same physical node on a subdomain and on its round-r neighbour; only the first iface_count slots are shared. `iface_count`: equal on both sides of a pair, 0 where the round has no neighbour. `face_nodes`: face 0 is the lower face, face 1 the upper one; slot k of the upper face of slab s is slot k of the lower face of slab s + 1 at the same index along sub. `owner_ids`: for a used slot, one of the two subdomains of the pair, the same on both sides; for an unused slot, the subdomain's own index.
All inputs are finite; a program needn't handle non-finite values.
Results may differ from a plain program's by a relative error of at most 0.0003.
Values sent between devices are 32-bit elements; how exact they have to be, the bound alone decides.
A program may use at most 128 MiB of HBM per device.

v0:
```python
import jax
import jax.numpy as jnp
from jax import lax
from jax.sharding import PartitionSpec as P

EX = 4
EY = 4
EZ = 127
IFACE = 256
ROUNDS = 3
KRYLOV = 3
CASES = 2
ELEMS = 2032
NODES = 3200


PRECISE = lax.Precision.HIGHEST
BRINKMAN_MAX = 4.0
RAMP_PARAM = 0.1


def swapped(block, axis, bit):
    count = lax.axis_size(axis)
    route = []
    for low in range(count):
        high = low | 1 << bit
        if high != low and high < count:
            route += [(low, high), (high, low)]
    return lax.ppermute(block, axis, route)


def extended_2(block, sides, width):
    for axis, dim in sides:
        count = lax.axis_size(axis)
        forward = [(i, i + 1) for i in range(count - 1)]
        backward = [(target, source) for source, target in forward]
        low = lax.ppermute(
            lax.slice_in_dim(block, block.shape[dim] - width, None, axis=dim), axis, forward
        )
        high = lax.ppermute(lax.slice_in_dim(block, 0, width, axis=dim), axis, backward)
        block = jnp.concatenate([low, block, high], axis=dim)
    return block


def corner_offsets(corner):
    return (corner // 4, corner // 2 % 2, corner % 2)


def element_vectors(field):
    channels = field.shape[0]
    node_grid = field.reshape(channels, EX + 1, EY + 1, EZ + 1)
    corner_list = []
    for corner in range(8):
        shift_x, shift_y, shift_z = corner_offsets(corner)
        window = node_grid[
            :, shift_x : shift_x + EX, shift_y : shift_y + EY, shift_z : shift_z + EZ
        ]
        corner_list.append(window.reshape(channels, ELEMS))
    return jnp.stack(corner_list, axis=1)


def node_sums(element_out):
    channels = element_out.shape[0]
    summed = jnp.zeros((channels, EX + 1, EY + 1, EZ + 1), jnp.float32)
    for corner in range(8):
        shift_x, shift_y, shift_z = corner_offsets(corner)
        corner_block = element_out[:, corner].reshape(channels, EX, EY, EZ)
        summed = summed + jnp.pad(
            corner_block,
            ((0, 0), (shift_x, 1 - shift_x), (shift_y, 1 - shift_y), (shift_z, 1 - shift_z)),
        )
    return summed.reshape(channels, NODES)


def brinkman_of(design):
    return BRINKMAN_MAX * RAMP_PARAM * (1.0 - design) / (RAMP_PARAM + design)


def adjoint_terms(state, brinkman, viscous_block, brinkman_block, coupling, stabilization):
    values = element_vectors(state).reshape(CASES, 32, ELEMS)
    velocity = values[:, :24]
    pressure = values[:, 24:]
    out_velocity = jnp.einsum("ij,cie->cje", viscous_block, velocity, precision=PRECISE)
    out_velocity = out_velocity + brinkman * jnp.einsum(
        "ij,cie->cje", brinkman_block, velocity, precision=PRECISE
    )
    out_velocity = out_velocity + jnp.einsum("kj,cke->cje", coupling, pressure, precision=PRECISE)
    out_pressure = jnp.einsum("kj,cje->cke", coupling, velocity, precision=PRECISE) - jnp.einsum(
        "lk,cle->cke", stabilization, pressure, precision=PRECISE
    )
    element_out = jnp.concatenate([out_velocity, out_pressure], axis=1).reshape(CASES * 4, 8, ELEMS)
    return node_sums(element_out)


def divergence_terms(velocity_nodes, coupling):
    element_vel = element_vectors(velocity_nodes).reshape(CASES, 24, ELEMS)
    return node_sums(jnp.einsum("kj,cje->cke", coupling, element_vel, precision=PRECISE))


def gradient_terms(pressure_nodes, coupling):
    element_pre = element_vectors(pressure_nodes)
    element_out = jnp.einsum("kj,cke->cje", coupling, element_pre, precision=PRECISE).reshape(
        CASES * 3, 8, ELEMS
    )
    return node_sums(element_out)


def diagonal_terms(brinkman, viscous_block, brinkman_block):
    diag_elem = (
        jnp.diagonal(viscous_block)[:, None]
        + jnp.diagonal(brinkman_block)[:, None] * brinkman[None, :]
    )
    return node_sums(diag_elem.reshape(3, 8, ELEMS))


def schur_terms(diag_nodes, coupling, stabilization):
    inverse = 1.0 / element_vectors(diag_nodes).reshape(24, ELEMS)
    schur_elem = (
        jnp.einsum("kj,je->ke", coupling * coupling, inverse, precision=PRECISE)
        + jnp.diagonal(stabilization)[:, None]
    )
    return node_sums(schur_elem[None])


def node_weights(iface_nodes, not_owned, lower_face, lower_lost):
    weights = jnp.ones((NODES,), jnp.float32)
    for matching in range(ROUNDS):
        keep = jnp.where(not_owned[matching], 0.0, 1.0).astype(weights.dtype)
        weights = weights.at[iface_nodes[matching]].multiply(keep)
    return weights.at[lower_face].multiply(jnp.where(lower_lost, 0.0, 1.0).astype(weights.dtype))


def assemble(partial_sums, layout):
    iface_nodes, iface_count, neighbours, face_nodes = layout
    slot_ids = jnp.arange(IFACE, dtype=jnp.int32)
    slot_valid = (slot_ids[None, :] < iface_count[:, None]).astype(jnp.float32)
    outgoing = jnp.stack(
        [
            partial_sums[:, iface_nodes[matching]] * slot_valid[matching][None, :]
            for matching in range(ROUNDS)
        ]
    )
    present = (neighbours >= 0).astype(jnp.float32)
    incoming = jnp.stack(
        [swapped(outgoing[matching], "sub", matching) for matching in range(ROUNDS)]
    )
    incoming = incoming * present[:, None, None]
    face_out = jnp.stack([partial_sums[:, face_nodes[0]], partial_sums[:, face_nodes[1]]])
    extended = extended_2(face_out, (("slab", 0),), 1)
    summed = partial_sums
    for matching in range(ROUNDS):
        summed = summed.at[:, iface_nodes[matching]].add(incoming[matching])
    summed = summed.at[:, face_nodes[0]].add(extended[0])
    return summed.at[:, face_nodes[1]].add(extended[3])


def weighted_norms(vectors, weights):
    return lax.psum(jnp.sum(weights * vectors * vectors, axis=(1, 2)), ("sub", "slab"))


def triangular_solves(factor, target):
    middle = []
    for row_index in range(KRYLOV):
        remainder = target[:, row_index] - sum(
            (factor[:, row_index, col_index] * middle[col_index] for col_index in range(row_index))
        )
        middle.append(remainder / factor[:, row_index, row_index])
    result = [None] * KRYLOV
    for row_index in reversed(range(KRYLOV)):
        remainder = middle[row_index] - sum(
            (
                factor[:, col_index, row_index] * result[col_index]
                for col_index in range(row_index + 1, KRYLOV)
            )
        )
        result[row_index] = remainder / factor[:, row_index, row_index]
    return jnp.stack(result, axis=1)


def per_device(
    adjoint_load,
    design,
    viscous_block,
    brinkman_block,
    coupling,
    stabilization,
    neighbours,
    iface_nodes,
    iface_count,
    face_nodes,
    owner_ids,
):
    layout = (iface_nodes[0, 0], iface_count[0, 0], neighbours[0, 0], face_nodes[0, 0])
    brinkman = brinkman_of(design[0, 0])
    sub_index = lax.axis_index("sub")
    slab_index = lax.axis_index("slab")
    slot_ids = jnp.arange(IFACE, dtype=jnp.int32)
    not_owned = (slot_ids[None, :] < iface_count[0, 0][:, None]) & (owner_ids[0, 0] != sub_index)
    weights = node_weights(iface_nodes[0, 0], not_owned, face_nodes[0, 0, 0], slab_index > 0)
    owned_load = (adjoint_load[0, 0] * weights).reshape(CASES * 4, NODES)
    assembled = assemble(
        jnp.concatenate(
            [owned_load, diagonal_terms(brinkman, viscous_block, brinkman_block)], axis=0
        ),
        layout,
    )
    start_vec = assembled[: CASES * 4].reshape(CASES, 4, NODES)
    diag_nodes = assembled[CASES * 4 :]
    schur_diag = assemble(schur_terms(diag_nodes, coupling, stabilization), layout)[0]
    start_norm = jnp.sqrt(weighted_norms(start_vec, weights))
    krylov_basis = [start_vec / start_norm[:, None, None]]
    hessenberg = jnp.zeros((CASES, KRYLOV + 1, KRYLOV), jnp.float32)
    directions = []
    for krylov_step in range(KRYLOV):
        precondition_vector = krylov_basis[-1]
        velocity_guess = precondition_vector[:, :3] / diag_nodes[None]
        divergence = assemble(
            divergence_terms(velocity_guess.reshape(CASES * 3, NODES), coupling), layout
        )
        pressure = (divergence - precondition_vector[:, 3]) / schur_diag[None]
        gradient = assemble(gradient_terms(pressure, coupling), layout).reshape(CASES, 3, NODES)
        velocity = velocity_guess - gradient / diag_nodes[None]
        direction = jnp.concatenate([velocity, pressure[:, None]], axis=1)
        directions.append(direction)
        image_part = adjoint_terms(
            direction.reshape(CASES * 4, NODES),
            brinkman,
            viscous_block,
            brinkman_block,
            coupling,
            stabilization,
        )
        product_vec = assemble(image_part, layout).reshape(CASES, 4, NODES)
        local_heights = jnp.stack(
            [jnp.sum(weights * vector * product_vec, axis=(1, 2)) for vector in krylov_basis],
            axis=1,
        )
        local_square = jnp.sum(weights * product_vec * product_vec, axis=(1, 2))
        heights, squared = lax.psum((local_heights, local_square), ("sub", "slab"))
        length = jnp.sqrt(squared - jnp.sum(heights * heights, axis=1))
        for basis_index in range(len(krylov_basis)):
            product_vec = (
                product_vec - heights[:, basis_index, None, None] * krylov_basis[basis_index]
            )
        hessenberg = hessenberg.at[:, : krylov_step + 1, krylov_step].set(heights)
        hessenberg = hessenberg.at[:, krylov_step + 1, krylov_step].set(length)
        krylov_basis.append(product_vec / length[:, None, None])
    normal_matrix = jnp.einsum("cij,cik->cjk", hessenberg, hessenberg, precision=PRECISE)
    target = start_norm[:, None] * hessenberg[:, 0, :]
    factor = jnp.linalg.cholesky(normal_matrix)
    coefficients = triangular_solves(factor, target)
    solution = sum(
        (
            coefficients[:, krylov_step, None, None] * directions[krylov_step]
            for krylov_step in range(KRYLOV)
        )
    )
    return (solution[None, None], coefficients)


def solution(mesh):
    placed = (
        P("slab", "sub", None, None, None),
        P("slab", "sub", None),
        P(),
        P(),
        P(),
        P(),
        P("slab", "sub", None),
        P("slab", "sub", None, None),
        P("slab", "sub", None),
        P("slab", "sub", None, None),
        P("slab", "sub", None, None),
    )
    return jax.shard_map(
        per_device,
        mesh=mesh,
        in_specs=placed,
        out_specs=(P("slab", "sub", None, None, None), P()),
        check_vma=False,
    )
```

profile of v0, /device:TPU:0, one launch (start us, length us, event | category | flops | bytes accessed | tf_op | source)
XLA Modules:
  0.0 715.5 jit_solution(7968014166761074142)
XLA Ops:
  17.1 4.1 collective-permute-start.2
  50.5 41.6 %psum.49 = f32[2]{0:T(128)S(1)} all-reduce(f32[2]{0:T(128)S(1)} %reduce_sum.144), channel_id=1, replica_groups=mesh['sub'=8,'slab'=4] {'sub','slab'}, use_global_device_ids=true, to_apply=%region_11.12 | all-reduce | flops 2 | bytes 16 | tf_op jit(solution)/shard_map/psum | solution.py:158
  176.3 4.1 scatter_custom_fusion.13
  195.3 4.0 pad_add_fusion.5
  223.2 4.0 scatter_custom_fusion.22
  227.3 4.2 scatter_custom_fusion.23
  250.2 4.0 pad_add_fusion.4
  263.4 4.2 collective-permute-start.23
  281.6 4.0 scatter_custom_fusion.28
  286.8 42.9 %all-reduce.91 = (f32[2]{0:T(128)S(1)}, f32[2,1]{0,1:T(1,128)S(1)}) all-reduce(f32[2]{0:T(128)S(1)} %reduce_sum.153, f32[2,1]{0,1:T(1,128)S(1)} %bitcast.879), channel_id=1, replica_groups=mesh['sub'=8,'slab'=4] {'sub','slab'}, use_global_device_ids=true, to_apply=%region_37.38 | all-reduce | flops 4 | bytes 32 | tf_op jit(solution)/shard_map/psum | solution.py:239
  359.1 4.2 scatter_custom_fusion.33
  378.2 4.0 pad_add_fusion.3
  392.1 4.5 collective-permute-start.33
  410.7 4.4 scatter_custom_fusion.38
  433.8 4.0 pad_add_fusion.2
  448.6 4.3 collective-permute-start.38
  472.3 43.2 %all-reduce.90 = (f32[2,2]{0,1:T(2,128)S(1)}, f32[2]{0:T(128)S(1)}) all-reduce(f32[2,2]{0,1:T(2,128)S(1)} %pad_maximum_fusion.8, f32[2]{0:T(128)S(1)} %reduce_sum.202), channel_id=1, replica_groups=mesh['sub'=8,'slab'=4] {'sub','slab'}, use_global_device_ids=true, to_apply=%region_57.58 | all-reduce | flops 6 | bytes 48 | tf_op jit(solution)/shard_map/psum | solution.py:239
  548.2 4.4 scatter_custom_fusion.48
  567.4 4.0 pad_add_fusion.1
  581.3 4.4 collective-permute-start.48
  600.4 4.3 scatter_custom_fusion.53
  623.4 4.1 pad_add_fusion
  640.2 4.2 collective-permute-start.53
  665.9 42.5 %all-reduce.89 = (f32[2,3]{0,1:T(4,128)S(1)}, f32[2]{0:T(128)S(1)}) all-reduce(f32[2,3]{0,1:T(4,128)S(1)} %pad_maximum_fusion.7, f32[2]{0:T(128)S(1)} %reduce_sum.215), channel_id=1, replica_groups=mesh['sub'=8,'slab'=4] {'sub','slab'}, use_global_device_ids=true, to_apply=%region_84.85 | all-reduce | flops 8 | bytes 64 | tf_op jit(solution)/shard_map/psum | solution.py:239
  (1021 shorter events, 455.5 us)
Async XLA Ops:
  17.1 15.6 %collective-permute-start.2 = (f32[11,256]{0,1:T(8,128)S(1)}, f32[11,256]{0,1:T(8,128)S(1)}, u32[]{:S(2)}, u32[]{:S(2)}) collective-permute-start(f32[11,256]{0,1:T(8,128)S(1)} %multiply_bitcast_fusion.27), channel_id=1, source_target_pairs={{0,16},{16,0},{4,20},{20,4},{8,24},{24,8},{12,28},{28,12},{1,17},{... | collective-permute-start | bytes 33800 | tf_op jit(solution)/shard_map/ppermute | solution.py:29
  27.1 14.1 %collective-permute-start.3 = (f32[1,11,512]{1,2,0:T(8,128)S(1)}, f32[1,11,512]{1,2,0:T(8,128)S(1)}, u32[]{:S(2)}, u32[]{:S(2)}) collective-permute-start(f32[1,11,512]{1,2,0:T(8,128)S(1)} %bitcast.840), channel_id=1, source_target_pairs={{0,1},{1,2},{2,3},{4,5},{5,6},{6,7},{8,9},{9,10},{10,11},{12,13},{... | collective-permute-start | bytes 67592 | tf_op jit(solution)/shard_map/ppermute | solution.py:37
  29.5 15.7 %collective-permute-start.4 = (f32[1,11,512]{1,2,0:T(8,128)S(1)}, f32[1,11,512]{1,2,0:T(8,128)S(1)}, u32[]{:S(2)}, u32[]{:S(2)}) collective-permute-start(f32[1,11,512]{1,2,0:T(8,128)S(1)} %bitcast.839), channel_id=1, source_target_pairs={{1,0},{2,1},{3,2},{5,4},{6,5},{7,6},{9,8},{10,9},{11,10},{13,12},{... | collective-permute-start | bytes 67592 | tf_op jit(solution)/shard_map/ppermute | solution.py:40
  133.2 19.5 %collective-permute-start.7 = (f32[2,256]{0,1:T(8,128)S(1)}, f32[2,256]{0,1:T(8,128)S(1)}, u32[]{:S(2)}, u32[]{:S(2)}) collective-permute-start(f32[2,256]{0,1:T(8,128)S(1)} %multiply_bitcast_fusion.24), channel_id=1, source_target_pairs={{0,16},{16,0},{4,20},{20,4},{8,24},{24,8},{12,28},{28,12},{1,17},{... | collective-permute-start | bytes 6152 | tf_op jit(solution)/shard_map/ppermute | solution.py:29
  140.4 15.6 %collective-permute-start.6 = (f32[2,256]{0,1:T(8,128)S(1)}, f32[2,256]{0,1:T(8,128)S(1)}, u32[]{:S(2)}, u32[]{:S(2)}) collective-permute-start(f32[2,256]{0,1:T(8,128)S(1)} %multiply_bitcast_fusion.25), channel_id=1, source_target_pairs={{0,8},{8,0},{4,12},{12,4},{16,24},{24,16},{20,28},{28,20},{1,9},{9... | collective-permute-start | bytes 6152 | tf_op jit(solution)/shard_map/ppermute | solution.py:29
  141.6 15.8 %collective-permute-start.5 = (f32[2,256]{0,1:T(8,128)S(1)}, f32[2,256]{0,1:T(8,128)S(1)}, u32[]{:S(2)}, u32[]{:S(2)}) collective-permute-start(f32[2,256]{0,1:T(8,128)S(1)} %multiply_bitcast_fusion.26), channel_id=1, source_target_pairs={{0,4},{4,0},{8,12},{12,8},{16,20},{20,16},{24,28},{28,24},{1,5},{5... | collective-permute-start | bytes 6152 | tf_op jit(solution)/shard_map/ppermute | solution.py:29
  143.9 28.4 %collective-permute-start.8 = (f32[1,2,512]{1,2,0:T(8,128)}, f32[1,2,512]{1,2,0:T(8,128)S(1)}, u32[]{:S(2)}, u32[]{:S(2)}) collective-permute-start(f32[1,2,512]{1,2,0:T(8,128)} %bitcast.54), channel_id=1, source_target_pairs={{0,1},{1,2},{2,3},{4,5},{5,6},{6,7},{8,9},{9,10},{10,11},{12,13},{... | collective-permute-start | bytes 12296 | tf_op jit(solution)/shard_map/ppermute | solution.py:37
  145.2 31.1 %collective-permute-start.9 = (f32[1,2,512]{1,2,0:T(8,128)}, f32[1,2,512]{1,2,0:T(8,128)S(1)}, u32[]{:S(2)}, u32[]{:S(2)}) collective-permute-start(f32[1,2,512]{1,2,0:T(8,128)} %bitcast.880), channel_id=1, source_target_pairs={{1,0},{2,1},{3,2},{5,4},{6,5},{7,6},{9,8},{10,9},{11,10},{13,12},{... | collective-permute-start | bytes 12296 | tf_op jit(solution)/shard_map/ppermute | solution.py:40
  213.1 14.2 %collective-permute-start.19 = (f32[1,6,512]{1,2,0:T(8,128)}, f32[1,6,512]{1,2,0:T(8,128)S(1)}, u32[]{:S(2)}, u32[]{:S(2)}) collective-permute-start(f32[1,6,512]{1,2,0:T(8,128)} %bitcast.869), channel_id=1, source_target_pairs={{1,0},{2,1},{3,2},{5,4},{6,5},{7,6},{9,8},{10,9},{11,10},{13,12},{... | collective-permute-start | bytes 36872 | tf_op jit(solution)/shard_map/ppermute | solution.py:40
  263.4 14.1 %collective-permute-start.23 = (f32[1,8,512]{1,2,0:T(8,128)}, f32[1,8,512]{1,2,0:T(8,128)S(1)}, u32[]{:S(2)}, u32[]{:S(2)}) collective-permute-start(f32[1,8,512]{1,2,0:T(8,128)} %bitcast.125), channel_id=1, source_target_pairs={{0,1},{1,2},{2,3},{4,5},{5,6},{6,7},{8,9},{9,10},{10,11},{12,13},{... | collective-permute-start | bytes 49160 | tf_op jit(solution)/shard_map/ppermute | solution.py:37
  267.6 13.9 %collective-permute-start.24 = (f32[1,8,512]{1,2,0:T(8,128)}, f32[1,8,512]{1,2,0:T(8,128)S(1)}, u32[]{:S(2)}, u32[]{:S(2)}) collective-permute-start(f32[1,8,512]{1,2,0:T(8,128)} %bitcast.872), channel_id=1, source_target_pairs={{1,0},{2,1},{3,2},{5,4},{6,5},{7,6},{9,8},{10,9},{11,10},{13,12},{... | collective-permute-start | bytes 49160 | tf_op jit(solution)/shard_map/ppermute | solution.py:40
  345.3 13.8 %collective-permute-start.29 = (f32[1,2,512]{1,2,0:T(8,128)}, f32[1,2,512]{1,2,0:T(8,128)S(1)}, u32[]{:S(2)}, u32[]{:S(2)}) collective-permute-start(f32[1,2,512]{1,2,0:T(8,128)} %bitcast.882), channel_id=1, source_target_pairs={{1,0},{2,1},{3,2},{5,4},{6,5},{7,6},{9,8},{10,9},{11,10},{13,12},{... | collective-permute-start | bytes 12296 | tf_op jit(solution)/shard_map/ppermute | solution.py:40
  392.1 14.5 %collective-permute-start.33 = (f32[1,6,512]{1,2,0:T(8,128)}, f32[1,6,512]{1,2,0:T(8,128)S(1)}, u32[]{:S(2)}, u32[]{:S(2)}) collective-permute-start(f32[1,6,512]{1,2,0:T(8,128)} %bitcast.178), channel_id=1, source_target_pairs={{0,1},{1,2},{2,3},{4,5},{5,6},{6,7},{8,9},{9,10},{10,11},{12,13},{... | collective-permute-start | bytes 36872 | tf_op jit(solution)/shard_map/ppermute | solution.py:37
  396.6 14.1 %collective-permute-start.34 = (f32[1,6,512]{1,2,0:T(8,128)}, f32[1,6,512]{1,2,0:T(8,128)S(1)}, u32[]{:S(2)}, u32[]{:S(2)}) collective-permute-start(f32[1,6,512]{1,2,0:T(8,128)} %bitcast.870), channel_id=1, source_target_pairs={{1,0},{2,1},{3,2},{5,4},{6,5},{7,6},{9,8},{10,9},{11,10},{13,12},{... | collective-permute-start | bytes 36872 | tf_op jit(solution)/shard_map/ppermute | solution.py:40
  440.6 13.6 %collective-permute-start.37 = (f32[8,256]{0,1:T(8,128)S(1)}, f32[8,256]{0,1:T(8,128)S(1)}, u32[]{:S(2)}, u32[]{:S(2)}) collective-permute-start(f32[8,256]{0,1:T(8,128)S(1)} %multiply_bitcast_fusion.9), channel_id=1, source_target_pairs={{0,16},{16,0},{4,20},{20,4},{8,24},{24,8},{12,28},{28,12},{1,17},{... | collective-permute-start | bytes 24584 | tf_op jit(solution)/shard_map/ppermute | solution.py:29
  448.6 14.1 %collective-permute-start.38 = (f32[1,8,512]{1,2,0:T(8,128)}, f32[1,8,512]{1,2,0:T(8,128)S(1)}, u32[]{:S(2)}, u32[]{:S(2)}) collective-permute-start(f32[1,8,512]{1,2,0:T(8,128)} %bitcast.204), channel_id=1, source_target_pairs={{0,1},{1,2},{2,3},{4,5},{5,6},{6,7},{8,9},{9,10},{10,11},{12,13},{... | collective-permute-start | bytes 49160 | tf_op jit(solution)/shard_map/ppermute | solution.py:37
  452.9 13.9 %collective-permute-start.39 = (f32[1,8,512]{1,2,0:T(8,128)}, f32[1,8,512]{1,2,0:T(8,128)S(1)}, u32[]{:S(2)}, u32[]{:S(2)}) collective-permute-start(f32[1,8,512]{1,2,0:T(8,128)} %bitcast.873), channel_id=1, source_target_pairs={{1,0},{2,1},{3,2},{5,4},{6,5},{7,6},{9,8},{10,9},{11,10},{13,12},{... | collective-permute-start | bytes 49160 | tf_op jit(solution)/shard_map/ppermute | solution.py:40
  534.4 13.8 %collective-permute-start.44 = (f32[1,2,512]{1,2,0:T(8,128)}, f32[1,2,512]{1,2,0:T(8,128)S(1)}, u32[]{:S(2)}, u32[]{:S(2)}) collective-permute-start(f32[1,2,512]{1,2,0:T(8,128)} %bitcast.881), channel_id=1, source_target_pairs={{1,0},{2,1},{3,2},{5,4},{6,5},{7,6},{9,8},{10,9},{11,10},{13,12},{... | collective-permute-start | bytes 12296 | tf_op jit(solution)/shard_map/ppermute | solution.py:40
  581.3 15.0 %collective-permute-start.48 = (f32[1,6,512]{1,2,0:T(8,128)}, f32[1,6,512]{1,2,0:T(8,128)S(1)}, u32[]{:S(2)}, u32[]{:S(2)}) collective-permute-start(f32[1,6,512]{1,2,0:T(8,128)} %bitcast.259), channel_id=1, source_target_pairs={{0,1},{1,2},{2,3},{4,5},{5,6},{6,7},{8,9},{9,10},{10,11},{12,13},{... | collective-permute-start | bytes 36872 | tf_op jit(solution)/shard_map/ppermute | solution.py:37
  585.7 14.6 %collective-permute-start.49 = (f32[1,6,512]{1,2,0:T(8,128)}, f32[1,6,512]{1,2,0:T(8,128)S(1)}, u32[]{:S(2)}, u32[]{:S(2)}) collective-permute-start(f32[1,6,512]{1,2,0:T(8,128)} %bitcast.871), channel_id=1, source_target_pairs={{1,0},{2,1},{3,2},{5,4},{6,5},{7,6},{9,8},{10,9},{11,10},{13,12},{... | collective-permute-start | bytes 36872 | tf_op jit(solution)/shard_map/ppermute | solution.py:40
  630.2 15.5 %collective-permute-start.52 = (f32[8,256]{0,1:T(8,128)S(1)}, f32[8,256]{0,1:T(8,128)S(1)}, u32[]{:S(2)}, u32[]{:S(2)}) collective-permute-start(f32[8,256]{0,1:T(8,128)S(1)} %multiply_bitcast_fusion), channel_id=1, source_target_pairs={{0,16},{16,0},{4,20},{20,4},{8,24},{24,8},{12,28},{28,12},{1,17},{... | collective-permute-start | bytes 24584 | tf_op jit(solution)/shard_map/ppermute | solution.py:29
  631.3 14.5 %collective-permute-start.51 = (f32[8,256]{0,1:T(8,128)S(1)}, f32[8,256]{0,1:T(8,128)}, u32[]{:S(2)}, u32[]{:S(2)}) collective-permute-start(f32[8,256]{0,1:T(8,128)S(1)} %multiply_bitcast_fusion.1), channel_id=1, source_target_pairs={{0,8},{8,0},{4,12},{12,4},{16,24},{24,16},{20,28},{28,20},{1,9},{9... | collective-permute-start | bytes 24584 | tf_op jit(solution)/shard_map/ppermute | solution.py:29
  640.2 16.0 %collective-permute-start.53 = (f32[1,8,512]{1,2,0:T(8,128)}, f32[1,8,512]{1,2,0:T(8,128)S(1)}, u32[]{:S(2)}, u32[]{:S(2)}) collective-permute-start(f32[1,8,512]{1,2,0:T(8,128)} %bitcast.285), channel_id=1, source_target_pairs={{0,1},{1,2},{2,3},{4,5},{5,6},{6,7},{8,9},{9,10},{10,11},{12,13},{... | collective-permute-start | bytes 49160 | tf_op jit(solution)/shard_map/ppermute | solution.py:37
  644.4 15.8 %collective-permute-start.54 = (f32[1,8,512]{1,2,0:T(8,128)}, f32[1,8,512]{1,2,0:T(8,128)S(1)}, u32[]{:S(2)}, u32[]{:S(2)}) collective-permute-start(f32[1,8,512]{1,2,0:T(8,128)} %bitcast.868), channel_id=1, source_target_pairs={{1,0},{2,1},{3,2},{5,4},{6,5},{7,6},{9,8},{10,9},{11,10},{13,12},{... | collective-permute-start | bytes 49160 | tf_op jit(solution)/shard_map/ppermute | solution.py:40
  (142 other events, 3164.3 us)
where the time goes:
time: 726 us; the launch traced here: 715 us
  other arithmetic  224 us (31%)
  local copies, waits for them, and re-layouts  211 us (29%)
  blocking collectives  170 us (23%)
  starting transfers between devices  94.4 us (13%)
  matrix products  9.5 us (1%)
    psum x3, blocking collectives, per_device(): heights, squared = lax.psum((local_heights, local_square), ('sub', 'slab'))  129 us
    scatter-add x33, other arithmetic, assemble(): summed = summed.at[:, iface_nodes[matching]].add(incoming[matching])  83.8 us
    another operation x136, local copies, waits for them, and re-layouts, node_sums(): corner_block = element_out[:, corner].reshape(channels, EX, EY, EZ)  72.7 us
    ppermute x33, starting transfers between devices, swapped(): return lax.ppermute(block, axis, route)  46.7 us
    scatter-add x11, other arithmetic, assemble(): return summed.at[:, face_nodes[1]].add(extended[3])  45.1 us
    scatter-add x11, other arithmetic, assemble(): summed = summed.at[:, face_nodes[0]].add(extended[0])  43.5 us
    psum x1, blocking collectives, weighted_norms(): lax.psum(jnp.sum(weights * vectors * vectors, axis=(1, 2)), ('sub', 'slab'))  41.6 us
    ppermute x11, starting transfers between devices, extended_2(): lax.ppermute(lax.slice_in_dim(block, block.shape[dim] - width, None, axis...  33.5 us
  transfers between devices with their start and end apart: 55, of which 1 were waited for; matrix products, arithmetic and copies ran while one was open for 25% of the time, Pallas kernels for 0%

commit v1 on v0

v1 whole, which is shorter than its diff:
```python
import functools

import jax
import jax.numpy as jnp
from jax import lax
from jax.experimental import pallas as pl
from jax.experimental.pallas import tpu as pltpu
from jax.sharding import PartitionSpec as P

EX = 4
EY = 4
EZ = 127
IFACE = 256
FACE = 512
ROUNDS = 3
KRYLOV = 3
CASES = 2
ELEMS = 2032
NODES = 3200

LANES = 128
ROWS = NODES // LANES
CH = 8
SLOTS = ROUNDS * IFACE + 2 * FACE
BLOCKS = SLOTS // LANES
FACE_BLOCKS = FACE // LANES
IFACE_BLOCKS = IFACE // LANES
BIG = 8 * CH

GROUPS = ((0, 0), (0, 1), (1, 0))
DEPTH = BIG * len(GROUPS)
PARTS = 2

BRINKMAN_MAX = 4.0
RAMP_PARAM = 0.1
EXCHANGES = 2 + 3 * KRYLOV
REDUCTIONS = KRYLOV + 1
HIGH = lax.Precision.HIGHEST
MESH = pl.DeviceIdType.MESH


def dot(a, b, ca, cb):
    return lax.dot_general(
        a, b, (((ca,), (cb,)), ((), ())), precision=HIGH, preferred_element_type=jnp.float32
    )


def one_hot(rows, cols, field, per_field):
    i = lax.broadcasted_iota(jnp.int32, (rows, cols), 0) & (BIG - 1)
    j = lax.broadcasted_iota(jnp.int32, (rows, cols), 1)
    same = (i >> 3) == (j & 7)
    f = i & 3
    if per_field:
        match = (f == (j >> 3)) & (j < 24)
    else:
        match = (f == field) & (j < 8)
    return jnp.where(same & match, 1.0, 0.0).astype(jnp.float32)


def kernel(
    n_sub,
    n_slab,
    load_ref,
    design_ref,
    visc_ref,
    brink_ref,
    coup_ref,
    stab_ref,
    iface_ref,
    count_ref,
    face_ref,
    owner_ref,
    out_ref,
    coef_ref,
    lo_ref,
    hi_ref,
    inv_block,
    inv_lane,
    wt_ref,
    x_ref,
    y_ref,
    y2_ref,
    t_ref,
    p_ref,
    diag_ref,
    schur_ref,
    z_ref,
    v_ref,
    flat_ref,
    brk_ref,
    lhs_j,
    lhs_d,
    lhs_g,
    lhs_s,
    send_buf,
    recv_buf,
    sub_buf,
    pad_ref,
    mid_ref,
    mat_ref,
    sum_ref,
    slab_buf,
    send_sem,
    recv_sem,
    sub_send_sem,
    sub_recv_sem,
    slab_send_sem,
    slab_recv_sem,
):
    sub = lax.axis_index("sub")
    slab = lax.axis_index("slab")
    sub_peers = [lax.rem(sub + d, n_sub) for d in range(1, n_sub)]
    slab_peers = [lax.rem(slab + d, n_slab) for d in range(1, n_slab)]
    partners = [
        sub + (1 << r) * (1 - 2 * lax.rem(sub // (1 << r), 2)) for r in range(ROUNDS)
    ]
    below = lax.rem(slab + n_slab - 1, n_slab)
    above = lax.rem(slab + 1, n_slab)

    barrier = pltpu.get_barrier_semaphore()
    for peer in sub_peers:
        pl.semaphore_signal(barrier, inc=1, device_id={"sub": peer}, device_id_type=MESH)
    for peer in slab_peers:
        pl.semaphore_signal(barrier, inc=1, device_id={"slab": peer}, device_id_type=MESH)

    lane = lax.broadcasted_iota(jnp.int32, (CH, LANES), 1)
    chan = lax.broadcasted_iota(jnp.int32, (CH, LANES), 0)
    is_p = (chan & 3) == 3
    inside = lane < EZ

    idx_parts, used_parts, lost_parts = [], [], []
    counts = count_ref[0]
    for r in range(ROUNDS):
        idx_parts.append(iface_ref[0, 0, r : r + 1, :])
        slot = lax.broadcasted_iota(jnp.int32, (1, IFACE), 1)
        used = slot < counts[:, r : r + 1]
        other = owner_ref[0, 0, r : r + 1, :] != sub
        used_parts.append(jnp.where(used, 1.0, 0.0))
        lost_parts.append(jnp.where(used & other, 1.0, 0.0))
    for side in range(2):
        idx_parts.append(face_ref[0, 0, side : side + 1, :])
        linked = slab > 0 if side == 0 else slab < n_slab - 1
        flag = jnp.where(linked, 1.0, 0.0).astype(jnp.float32)
        used_parts.append(jnp.full((1, FACE), 1.0, jnp.float32) * flag)
        lost_parts.append(
            jnp.full((1, FACE), 1.0 if side == 0 else 0.0, jnp.float32) * flag
        )
    idx = jnp.concatenate(idx_parts, axis=1)
    used = jnp.concatenate(used_parts, axis=1)
    lost = jnp.concatenate(lost_parts, axis=1)
    hi = idx >> 7
    lo = idx & (LANES - 1)
    for k in range(BLOCKS):
        cols = slice(k * LANES, (k + 1) * LANES)
        lo_ref[k] = jnp.broadcast_to(lo[:, cols], (CH, LANES))
        hi_ref[k] = jnp.broadcast_to(hi[:, cols], (CH, LANES))

    slot = lax.broadcasted_iota(jnp.int32, (1, SLOTS), 1)
    block_of = ((slot >> 7) + 1).astype(jnp.float32) * used
    lane_of = (slot & (LANES - 1)).astype(jnp.float32) * used
    hot_hi = lax.broadcasted_iota(jnp.int32, (32, SLOTS), 0) == hi
    hot_lo = jnp.where(
        lax.broadcasted_iota(jnp.int32, (LANES, SLOTS), 0) == lo, 1.0, 0.0
    ).astype(jnp.bfloat16)

    def to_nodes(values):
        left = jnp.where(hot_hi, values, 0.0).astype(jnp.bfloat16)
        return lax.dot_general(
            left, hot_lo, (((1,), (1,)), ((), ())), preferred_element_type=jnp.float32
        )

    node_block = to_nodes(block_of).astype(jnp.int32)
    node_lane = to_nodes(lane_of).astype(jnp.int32)
    node_lost = to_nodes(lost)
    for r in range(ROWS):
        inv_block[r] = jnp.broadcast_to(node_block[r : r + 1], (CH, LANES))
        inv_lane[r] = jnp.broadcast_to(node_lane[r : r + 1], (CH, LANES))
        wt_ref[r] = jnp.broadcast_to(1.0 - node_lost[r : r + 1], (CH, LANES))

    for r in range(ROWS):
        cols = slice(r * LANES, (r + 1) * LANES)
        both = jnp.concatenate([load_ref[0, 0, 0, :, cols], load_ref[0, 0, 1, :, cols]], axis=0)
        y_ref[r] = both * wt_ref[r]

    flat_ref[...] = jnp.zeros_like(flat_ref)
    flat_ref[:, 0:ELEMS] = jnp.broadcast_to(design_ref[0], (CH, ELEMS))
    for i in range(EX * EY):
        here = flat_ref[:, i * LANES : (i + 1) * LANES]
        if i > 0:
            before = flat_ref[:, (i - 1) * LANES : i * LANES]
            here = jnp.where(lane < i, pltpu.roll(before, i, 1), pltpu.roll(here, i, 1))
        value = BRINKMAN_MAX * RAMP_PARAM * (1.0 - here) / (RAMP_PARAM + here)
        brk_ref[i] = jnp.where(inside, value, 0.0)

    pad_ref[...] = jnp.zeros_like(pad_ref)
    for i, block in enumerate((visc_ref, brink_ref, coup_ref, stab_ref)):
        pad_ref[i, 0 : block.shape[0], 0 : block.shape[1]] = block[...]
    visc, brink, coup, stab = (pad_ref[i] for i in range(4))
    e_u = one_hot(BIG, LANES, 0, True)
    e_p = one_hot(BIG, LANES, 3, False)
    e_s = one_hot(BIG, LANES, 0, False)
    w_u = one_hot(DEPTH, LANES, 0, True)
    w_p = one_hot(DEPTH, LANES, 3, False)
    row_case = (lax.broadcasted_iota(jnp.int32, (BIG, DEPTH), 0) >> 2) & 1
    col = lax.broadcasted_iota(jnp.int32, (BIG, DEPTH), 1)
    same_case = row_case == ((col >> 2) & 1)
    first_part = jnp.zeros((BIG, DEPTH), jnp.bool_)
    for g, (part, _) in enumerate(GROUPS):
        if part == 0:
            first_part = first_part | ((col >> 6) == g)

    def split_matrix(matrix):
        mat_ref[...] = jnp.where(same_case, matrix, 0.0)
        matrix = mat_ref[...]
        head = matrix.astype(jnp.bfloat16).astype(jnp.float32)
        return jnp.where(first_part, head, matrix - head).astype(jnp.bfloat16)

    def expand(left, block, side, right):
        mid_ref[...] = dot(left, block, 1, side)
        return dot(mid_ref[...], right, 1, 1)

    big_d = expand(e_p, coup, 0, w_u)
    big_g = expand(e_u, coup, 1, w_p)
    big_b = expand(e_u, brink, 1, w_u)
    sum_ref[...] = big_d + big_g
    sum_ref[...] += expand(e_u, visc, 1, w_u)
    sum_ref[...] -= expand(e_p, stab, 1, w_p)
    lhs_j[0:BIG] = split_matrix(sum_ref[...])
    lhs_j[BIG : 2 * BIG] = split_matrix(big_b)
    lhs_d[...] = split_matrix(big_d)
    lhs_g[...] = split_matrix(big_g)
    lhs_s[...] = split_matrix(expand(e_s, coup * coup, 0, w_u))

    def diagonal(matrix, hot):
        size = matrix.shape[0]
        eye = lax.broadcasted_iota(jnp.int32, (size, size), 0) == lax.broadcasted_iota(
            jnp.int32, (size, size), 1
        )
        row = jnp.sum(jnp.where(eye, matrix, 0.0), axis=0, keepdims=True)
        column = jnp.sum(hot * row, axis=1, keepdims=True)
        return jnp.broadcast_to(column, (BIG, LANES))

    def node_rows(element_out, target):
        near = [None] * ROWS
        far = [None] * ROWS

        def put(store, at, value):
            store[at] = value if store[at] is None else store[at] + value

        for a in range(EX):
            blocks = element_out(a)
            for b in range(EY):
                for q in range(8):
                    at = (a + q // 4) * (EY + 1) + b + q // 2 % 2
                    put(far if q % 2 else near, at, blocks[b][q])
        for r in range(ROWS):
            target[r] = near[r] + pltpu.roll(far[r], 1, 1)

    def split_nodes(source):
        for r in range(ROWS):
            x = source(r)
            rest = jnp.concatenate(
                [
                    jnp.where(inside, x, 0.0),
                    jnp.where(inside, pltpu.roll(x, LANES - 1, 1), 0.0),
                ],
                axis=0,
            )
            for part in range(PARTS):
                head = rest.astype(jnp.bfloat16)
                t_ref[part, r * 16 : (r + 1) * 16] = head
                rest = rest - head.astype(jnp.float32)

    def product(lhs, a):
        columns = []
        for b in range(EY):
            pieces = []
            for _, part in GROUPS:
                for r in (a * (EY + 1) + b, (a + 1) * (EY + 1) + b):
                    pieces.append(t_ref[part, r * 16 : (r + 2) * 16])
            columns.append(jnp.concatenate(pieces, axis=0))
        return jnp.dot(
            lhs[...], jnp.concatenate(columns, axis=1), preferred_element_type=jnp.float32
        )

    def corner(out, b, q, base=0):
        return out[base + q * CH : base + (q + 1) * CH, b * LANES : (b + 1) * LANES]

    def plain(lhs):
        def element_out(a):
            out = product(lhs, a)
            return [[corner(out, b, q) for q in range(8)] for b in range(EY)]

        return element_out

    def adjoint(a):
        out = product(lhs_j, a)
        return [
            [
                corner(out, b, q) + brk_ref[a * EY + b] * corner(out, b, q, BIG)
                for q in range(8)
            ]
            for b in range(EY)
        ]

    def diag_out(a):
        return [
            [
                jnp.where(inside, diag_v[q * CH : (q + 1) * CH], 0.0)
                + diag_b[q * CH : (q + 1) * CH] * brk_ref[a * EY + b]
                for q in range(8)
            ]
            for b in range(EY)
        ]

    def copies(e):
        made = []
        for r in range(ROUNDS):
            part = pl.ds(r * IFACE_BLOCKS, IFACE_BLOCKS)
            made.append((part, part, {"sub": partners[r]}))
        base = ROUNDS * IFACE_BLOCKS
        low, high = pl.ds(base, FACE_BLOCKS), pl.ds(base + FACE_BLOCKS, FACE_BLOCKS)
        made.append((low, high, {"slab": below}))
        made.append((high, low, {"slab": above}))
        return [
            pltpu.make_async_remote_copy(
                src_ref=send_buf.at[e, src],
                dst_ref=recv_buf.at[e, dst],
                send_sem=send_sem.at[e, i],
                recv_sem=recv_sem.at[e, i],
                device_id=device,
                device_id_type=MESH,
            )
            for i, (src, dst, device) in enumerate(made)
        ]

    started = []

    def post(e, source):
        los = [lo_ref[k] for k in range(BLOCKS)]
        his = [hi_ref[k] for k in range(BLOCKS)]

        def body(r, found):
            row = source[r]
            return tuple(
                jnp.where(
                    his[k] == r,
                    jnp.take_along_axis(row, los[k], axis=1, mode="promise_in_bounds"),
                    found[k],
                )
                for k in range(BLOCKS)
            )

        zero = jnp.zeros((CH, LANES), jnp.float32)
        found = lax.fori_loop(0, ROWS, body, (zero,) * BLOCKS, unroll=5)
        for k in range(BLOCKS):
            send_buf[e, k] = found[k]
        for copy in copies(e):
            copy.start()
            started.append(copy)

    def arrive(e):
        for copy in copies(e):
            copy.wait_recv()

    def received(e, r):
        at = inv_block[r]
        lanes = inv_lane[r]
        total = jnp.zeros((CH, LANES), jnp.float32)
        for k in range(BLOCKS):
            value = jnp.take_along_axis(
                recv_buf[e, k], lanes, axis=1, mode="promise_in_bounds"
            )
            total = jnp.where(at == k + 1, value, total)
        return total

    def each_row(body, sums=0):
        zero = jnp.zeros((CH, LANES), jnp.float32)

        def step(r, carry):
            added = body(r)
            return tuple(c + t for c, t in zip(carry, added))

        return lax.fori_loop(0, ROWS, step, (zero,) * sums)

    def sub_copies(t):
        return [
            pltpu.make_async_remote_copy(
                src_ref=sub_buf.at[t, sub],
                dst_ref=sub_buf.at[t, sub],
                send_sem=sub_send_sem.at[t, d],
                recv_sem=sub_recv_sem.at[t, d],
                device_id={"sub": peer},
                device_id_type=MESH,
            )
            for d, peer in enumerate(sub_peers)
        ]

    def sub_arrivals(t):
        return [
            pltpu.make_async_copy(
                sub_buf.at[t, lax.rem(sub + n_sub - d, n_sub)],
                sub_buf.at[t, lax.rem(sub + n_sub - d, n_sub)],
                sub_recv_sem.at[t, d - 1],
            )
            for d in range(1, n_sub)
        ]

    def slab_copies(t):
        return [
            pltpu.make_async_remote_copy(
                src_ref=slab_buf.at[t, slab],
                dst_ref=slab_buf.at[t, slab],
                send_sem=slab_send_sem.at[t, d],
                recv_sem=slab_recv_sem.at[t, d],
                device_id={"slab": peer},
                device_id_type=MESH,
            )
            for d, peer in enumerate(slab_peers)
        ]

    def slab_arrivals(t):
        return [
            pltpu.make_async_copy(
                slab_buf.at[t, lax.rem(slab + n_slab - d, n_slab)],
                slab_buf.at[t, lax.rem(slab + n_slab - d, n_slab)],
                slab_recv_sem.at[t, d - 1],
            )
            for d in range(1, n_slab)
        ]

    def reduce_start(t, partial_sums):
        message = jnp.zeros((CH, LANES), jnp.float32)
        for i, value in enumerate(partial_sums):
            total = jnp.sum(value, axis=1, keepdims=True)
            message = jnp.where(lane == i, total, message)
        sub_buf[t, sub] = message
        for copy in sub_copies(t):
            copy.start()
            started.append(copy)

    def reduce_middle(t):
        for copy in sub_arrivals(t):
            copy.wait()
        total = sub_buf[t, 0]
        for i in range(1, n_sub):
            total = total + sub_buf[t, i]
        slab_buf[t, slab] = total
        for copy in slab_copies(t):
            copy.start()
            started.append(copy)

    def reduce_end(t, number):
        for copy in slab_arrivals(t):
            copy.wait()
        total = slab_buf[t, 0]
        for i in range(1, n_slab):
            total = total + slab_buf[t, i]
        first = jnp.sum(jnp.where(chan < 4, total, 0.0), axis=0, keepdims=True)
        second = jnp.sum(jnp.where(chan < 4, 0.0, total), axis=0, keepdims=True)
        total = jnp.where(chan < 4, first, second)
        return [
            jnp.broadcast_to(total[:, i : i + 1], (CH, LANES)) for i in range(number)
        ]

    pl.semaphore_wait(barrier, n_sub - 1 + n_slab - 1)

    post(0, y_ref)
    diag_v = diagonal(visc, e_u)
    diag_b = diagonal(brink, e_u)
    node_rows(diag_out, y2_ref)
    post(1, y2_ref)
    arrive(0)

    def load_row(r):
        value = y_ref[r] + received(0, r)
        x_ref[r] = value
        return (value * value * wt_ref[r],)

    (square,) = each_row(load_row, 1)
    reduce_start(0, [square])
    arrive(1)

    def diag_row(r):
        diag_ref[r] = jnp.where(is_p, 1.0, y2_ref[r] + received(1, r))
        return ()

    each_row(diag_row)

    heights = []
    start_norm = None
    exchange = 2
    for step in range(KRYLOV):
        split_nodes(lambda r: x_ref[r] / diag_ref[r])
        node_rows(plain(lhs_d), y_ref)
        if step == 0:
            diag_s = diagonal(stab, e_s)
            split_nodes(lambda r: 1.0 / diag_ref[r])

            def schur_out(a):
                out = product(lhs_s, a)
                return [
                    [
                        corner(out, b, q)
                        + jnp.where(inside, diag_s[q * CH : (q + 1) * CH], 0.0)
                        for q in range(8)
                    ]
                    for b in range(EY)
                ]

            node_rows(schur_out, y2_ref)
            for r in range(ROWS):
                y_ref[r] = y_ref[r] + y2_ref[r]
        post(exchange, y_ref)
        reduce_middle(step)
        arrive(exchange)

        def pressure_row(r, step=step, exchange=exchange):
            value = y_ref[r] + received(exchange, r)
            if step == 0:
                schur = jnp.where(is_p, pltpu.roll(value, 3, 0), 1.0)
                schur_ref[r] = schur
            else:
                schur = schur_ref[r]
            p_ref[r] = jnp.where(is_p, (value - x_ref[r]) / schur, 0.0)
            return ()

        each_row(pressure_row)
        split_nodes(lambda r: p_ref[r])
        node_rows(plain(lhs_g), y_ref)
        post(exchange + 1, y_ref)

        sums = reduce_end(step, step + 1)
        if step == 0:
            start_norm = jnp.sqrt(sums[0])
            height, length = [], start_norm
        else:
            height, squared = sums[:step], sums[step]
            length = jnp.sqrt(squared - sum(h * h for h in height))
            heights.append(height + [length])
        arrive(exchange + 1)

        def direction_row(r, step=step, exchange=exchange, height=height, length=length):
            x = x_ref[r]
            diag = diag_ref[r]
            value = y_ref[r] + received(exchange + 1, r)
            z = jnp.where(is_p, p_ref[r], x / diag - value / diag)
            for m, h in enumerate(height):
                z = z - h * z_ref[m, r]
                x = x - h * v_ref[m, r]
            z_ref[step, r] = z / length
            v_ref[step, r] = x / length
            return ()

        each_row(direction_row)
        split_nodes(lambda r: z_ref[step, r])
        node_rows(adjoint, y_ref)
        post(exchange + 2, y_ref)
        arrive(exchange + 2)

        def image_row(r, step=step, exchange=exchange):
            w = y_ref[r] + received(exchange + 2, r)
            x_ref[r] = w
            weighted = w * wt_ref[r]
            return tuple(v_ref[m, r] * weighted for m in range(step + 1)) + (w * weighted,)

        products = each_row(image_row, step + 2)
        reduce_start(step + 1, products)
        exchange += 3

    reduce_middle(KRYLOV)
    sums = reduce_end(KRYLOV, KRYLOV + 1)
    height, squared = sums[:KRYLOV], sums[KRYLOV]
    heights.append(height + [jnp.sqrt(squared - sum(h * h for h in height))])

    def normal(i, j):
        return sum(heights[i][m] * heights[j][m] for m in range(min(i, j) + 2))

    factor = [[None] * KRYLOV for _ in range(KRYLOV)]
    for i in range(KRYLOV):
        for j in range(i + 1):
            value = normal(i, j)
            for k in range(j):
                value = value - factor[i][k] * factor[j][k]
            factor[i][j] = jnp.sqrt(value) if i == j else value / factor[j][j]
    middle = []
    for i in range(KRYLOV):
        value = start_norm * heights[i][0]
        for k in range(i):
            value = value - factor[i][k] * middle[k]
        middle.append(value / factor[i][i])
    coefs = [None] * KRYLOV
    for i in reversed(range(KRYLOV)):
        value = middle[i]
        for k in range(i + 1, KRYLOV):
            value = value - factor[k][i] * coefs[k]
        coefs[i] = value / factor[i][i]

    table = jnp.zeros((CH, LANES), jnp.float32)
    for j in range(KRYLOV):
        table = jnp.where(lane == j, coefs[j], table)
    for case in range(CASES):
        coef_ref[case : case + 1, :] = table[case * 4 : case * 4 + 1, 0:KRYLOV]
    for r in range(ROWS):
        value = coefs[0] * z_ref[0, r]
        for j in range(1, KRYLOV):
            value = value + coefs[j] * z_ref[j, r]
        cols = slice(r * LANES, (r + 1) * LANES)
        for case in range(CASES):
            out_ref[0, 0, case, :, cols] = value[case * 4 : case * 4 + 4]

    for copy in started:
        copy.wait_send()


def per_device(
    n_sub,
    n_slab,
    adjoint_load,
    design,
    viscous_block,
    brinkman_block,
    coupling,
    stabilization,
    neighbours,
    iface_nodes,
    iface_count,
    face_nodes,
    owner_ids,
):
    tile = (CH, LANES)
    f32, i32, bf16 = jnp.float32, jnp.int32, jnp.bfloat16
    rows = (ROWS,) + tile
    dma = pltpu.SemaphoreType.DMA
    scratch = [
        pltpu.VMEM((BLOCKS,) + tile, i32),
        pltpu.VMEM((BLOCKS,) + tile, i32),
        pltpu.VMEM(rows, i32),
        pltpu.VMEM(rows, i32),
        pltpu.VMEM(rows, f32),
        pltpu.VMEM(rows, f32),
        pltpu.VMEM(rows, f32),
        pltpu.VMEM(rows, f32),
        pltpu.VMEM((PARTS, ROWS * 16, LANES), bf16),
        pltpu.VMEM(rows, f32),
        pltpu.VMEM(rows, f32),
        pltpu.VMEM(rows, f32),
        pltpu.VMEM((KRYLOV,) + rows, f32),
        pltpu.VMEM((KRYLOV,) + rows, f32),
        pltpu.VMEM((CH, EX * EY * LANES), f32),
        pltpu.VMEM((EX * EY,) + tile, f32),
        pltpu.VMEM((2 * BIG, DEPTH), bf16),
        pltpu.VMEM((BIG, DEPTH), bf16),
        pltpu.VMEM((BIG, DEPTH), bf16),
        pltpu.VMEM((BIG, DEPTH), bf16),
        pltpu.VMEM((EXCHANGES, BLOCKS) + tile, f32),
        pltpu.VMEM((EXCHANGES, BLOCKS) + tile, f32),
        pltpu.VMEM((REDUCTIONS, n_sub) + tile, f32),
        pltpu.VMEM((4, LANES, LANES), f32),
        pltpu.VMEM((BIG, LANES), f32),
        pltpu.VMEM((BIG, DEPTH), f32),
        pltpu.VMEM((BIG, DEPTH), f32),
        pltpu.VMEM((REDUCTIONS, n_slab) + tile, f32),
        dma((EXCHANGES, ROUNDS + 2)),
        dma((EXCHANGES, ROUNDS + 2)),
        dma((REDUCTIONS, n_sub - 1)),
        dma((REDUCTIONS, n_sub - 1)),
        dma((REDUCTIONS, n_slab - 1)),
        dma((REDUCTIONS, n_slab - 1)),
    ]
    vmem = pl.BlockSpec(memory_space=pltpu.VMEM)
    return pl.pallas_call(
        functools.partial(kernel, n_sub, n_slab),
        out_shape=(
            jax.ShapeDtypeStruct((1, 1, CASES, 4, NODES), f32),
            jax.ShapeDtypeStruct((CASES, KRYLOV), f32),
        ),
        in_specs=[vmem] * 10,
        out_specs=(vmem, vmem),
        scratch_shapes=scratch,
        compiler_params=pltpu.CompilerParams(
            collective_id=0, has_side_effects=True, vmem_limit_bytes=48 * 1024 * 1024
        ),
    )(
        adjoint_load,
        design,
        viscous_block,
        brinkman_block,
        coupling,
        stabilization,
        iface_nodes,
        iface_count,
        face_nodes,
        owner_ids,
    )


def solution(mesh):
    placed = (
        P("slab", "sub", None, None, None),
        P("slab", "sub", None),
        P(),
        P(),
        P(),
        P(),
        P("slab", "sub", None),
        P("slab", "sub", None, None),
        P("slab", "sub", None),
        P("slab", "sub", None, None),
        P("slab", "sub", None, None),
    )
    return jax.shard_map(
        functools.partial(per_device, mesh.shape["sub"], mesh.shape["slab"]),
        mesh=mesh,
        in_specs=placed,
        out_specs=(P("slab", "sub", None, None, None), P()),
        check_vma=False,
    )
```

time: 726 us -> 97.4 us (0.13); the launches traced: 715 us -> 97 us
  other arithmetic: 224 us -> 0 us
  local copies, waits for them, and re-layouts: 211 us -> 6.96 us
  blocking collectives: 170 us -> 0 us
  starting transfers between devices: 94.4 us -> 0 us
  Pallas kernels: 0 us -> 89.4 us
  matrix products: 9.5 us -> 0 us
    scatter-add x55 -> x0, other arithmetic: 172 us -> none  [the longest x33 83.8 us: assemble(): summed = summed.at[:, iface_nodes[matching]].add(incoming[matching])]
    psum x4 -> x0, blocking collectives: 170 us -> none  [the longest x3 129 us: per_device(): heights, squared = lax.psum((local_heights, local_square), ('sub', 'slab'))]
    ppermute x55 -> x0, starting transfers between devices: 94.4 us -> none  [the longest x33 46.7 us: swapped(): return lax.ppermute(block, axis, route)]
    another operation x268 -> x0, local copies, waits for them, and re-layouts: 93.4 us -> none  [the longest x136 72.7 us: node_sums(): corner_block = element_out[:, corner].reshape(channels, EX, EY, EZ)]
    pallas_call x0 -> x1, Pallas kernels: none -> 89.4 us  [per_device(): pl.pallas_call(functools.partial(kernel, n_sub, n_slab), out_shape=(jax.S...]
    gather x58 -> x0, local copies, waits for them, and re-layouts: 72.8 us -> none  [the longest x33 31.5 us: assemble(): partial_sums[:, iface_nodes[matching]] * slot_valid[matching][None, :]]
    add x13 -> x0, other arithmetic: 25.7 us -> none  [the longest x11 24.8 us: node_sums(): summed + jnp.pad(corner_block, ((0, 0), (shift_x, 1 - shift_x), (shift_y,...]
    slice x29 -> x0, local copies, waits for them, and re-layouts: 14.5 us -> none  [the longest x11 8.61 us: node_sums(): corner_block = element_out[:, corner].reshape(channels, EX, EY, EZ)]
  transfers between devices with their start and end apart: 55 -> 0, of which waited for: 1 -> 0; matrix products, arithmetic and copies ran while one was open for 25% -> 0% of each run, Pallas kernels for 0% -> 0%
where the time goes in v1:
time: 97.4 us; the launch traced here: 97 us
  Pallas kernels  89.4 us (92%)
  local copies, waits for them, and re-layouts  6.96 us (7%)
    pallas_call x1, Pallas kernels, per_device(): pl.pallas_call(functools.partial(kernel, n_sub, n_slab), out_shape=(jax.S...  89.4 us
    unnamed x20, local copies, waits for them, and re-layouts  6.96 us

profile of v1, /device:TPU:0, one launch (start us, length us, event | category | flops | bytes accessed | tf_op | source)
XLA Modules:
  0.0 97.0 jit_solution(4721094536251739155)
XLA Ops:
  0.6 0.0 copy-start.1
  0.6 0.7 copy.12.iface_ref
  1.3 0.0 copy-start.7
  1.3 0.7 copy.13.owner_ref
  2.0 0.0 copy-done.1
  2.0 0.0 copy-done.7
  2.0 0.0 copy-start
  2.0 0.9 copy-done
  2.9 0.0 copy-start.2
  2.9 0.7 copy-done.2
  3.6 0.0 copy-start.3
  3.6 0.7 copy-done.3
  4.3 0.0 copy-start.4
  4.3 0.7 copy-done.4
  5.0 0.0 copy-start.5
  5.0 0.7 copy-done.5
  5.7 0.0 copy-start.6
  5.7 0.7 copy-done.6
  6.4 89.4 %shard_map.113 = (f32[1,1,2,4,3200]{4,3,2,1,0:T(4,128)S(1)}, f32[2,3]{1,0:T(2,128)S(1)}) custom-call(f32[1,1,2,4,3200]{4,3,2,1,0:T(4,128)S(1)} %copy-done, f32[1,1,2032]{2,1,0:T(1,128)S(1)} %copy-done.3, f32[24,24]{1,0:T(8,128)S(1)} %copy-done.1, f32[24,24]{1,0:T(8,128)S(1)} %copy-done.2, f32[8,24]{1,0:T(8,128)S(1)} %copy-done.4, f32[8,8]{1,0:T(8,128)S(1)} %copy-done.5, ...), custom_call_target="tpu_custom_call" | custom-call | tf_op jit(solution)/shard_map/pallas_call | solution.py:672
  95.8 0.6 copy.16
  96.4 0.6 copy.17
Async XLA Ops:
  0.6 1.4 %copy-start.1 = (f32[24,24]{1,0:T(8,128)S(1)}, f32[24,24]{1,0:T(8,128)}, u32[]{:S(2)}) copy-start(f32[24,24]{1,0:T(8,128)} %visc_ref.1) | copy-start | bytes 6916
  1.3 0.7 copy-start.7
  2.0 0.9 copy-start
  2.9 0.7 copy-start.2
  3.6 0.7 copy-start.3
  4.3 0.7 copy-start.4
  5.0 0.7 copy-start.5
  5.7 0.7 copy-start.6

commit v2 on v1

--- a/solution.py
+++ b/solution.py
@@ -35,6 +35,8 @@
 RAMP_PARAM = 0.1
 EXCHANGES = 2 + 3 * KRYLOV
 REDUCTIONS = KRYLOV + 1
+UNROLL = ROWS
+INPUTS = 10
 HIGH = lax.Precision.HIGHEST
 MESH = pl.DeviceIdType.MESH
 
@@ -60,53 +62,67 @@
 def kernel(
     n_sub,
     n_slab,
-    load_ref,
-    design_ref,
-    visc_ref,
-    brink_ref,
-    coup_ref,
-    stab_ref,
-    iface_ref,
-    count_ref,
-    face_ref,
-    owner_ref,
-    out_ref,
-    coef_ref,
-    lo_ref,
-    hi_ref,
-    inv_block,
-    inv_lane,
-    wt_ref,
-    x_ref,
-    y_ref,
-    y2_ref,
-    t_ref,
-    p_ref,
-    diag_ref,
-    schur_ref,
-    z_ref,
-    v_ref,
-    flat_ref,
-    brk_ref,
-    lhs_j,
-    lhs_d,
-    lhs_g,
-    lhs_s,
-    send_buf,
-    recv_buf,
-    sub_buf,
-    pad_ref,
-    mid_ref,
-    mat_ref,
-    sum_ref,
-    slab_buf,
-    send_sem,
-    recv_sem,
-    sub_send_sem,
-    sub_recv_sem,
-    slab_send_sem,
-    slab_recv_sem,
+    *refs,
 ):
+    inputs = refs[:INPUTS]
+    (
+        out_ref,
+        coef_ref,
+        lo_ref,
+        hi_ref,
+        inv_block,
+        inv_lane,
+        wt_ref,
+        x_ref,
+        y_ref,
+        y2_ref,
+        t_ref,
+        p_ref,
+        diag_ref,
+        schur_ref,
+        z_ref,
+        v_ref,
+        flat_ref,
+        brk_ref,
+        lhs_j,
+        lhs_d,
+        lhs_g,
+        lhs_s,
+        send_buf,
+        recv_buf,
+        sub_buf,
+        pad_ref,
+        mid_ref,
+        mat_ref,
+        sum_ref,
+        slab_buf,
+        send_sem,
+        recv_sem,
+        sub_send_sem,
+        sub_recv_sem,
+        slab_send_sem,
+        slab_recv_sem,
+        in_sem,
+        *held,
+    ) = refs[INPUTS:]
+    fetches = [
+        pltpu.make_async_copy(source, target, in_sem.at[i])
+        for i, (source, target) in enumerate(zip(inputs, held))
+    ]
+    for fetch in fetches:
+        fetch.start()
+    (
+        load_ref,
+        design_ref,
+        visc_ref,
+        brink_ref,
+        coup_ref,
+        stab_ref,
+        iface_ref,
+        count_ref,
+        face_ref,
+        owner_ref,
+    ) = held
     sub = lax.axis_index("sub")
     slab = lax.axis_index("slab")
     sub_peers = [lax.rem(sub + d, n_sub) for d in range(1, n_sub)]
@@ -122,6 +138,9 @@
         pl.semaphore_signal(barrier, inc=1, device_id={"sub": peer}, device_id_type=MESH)
     for peer in slab_peers:
         pl.semaphore_signal(barrier, inc=1, device_id={"slab": peer}, device_id_type=MESH)
+
+    for fetch in fetches:
+        fetch.wait()
 
     lane = lax.broadcasted_iota(jnp.int32, (CH, LANES), 1)
     chan = lax.broadcasted_iota(jnp.int32, (CH, LANES), 0)
@@ -352,7 +371,7 @@
             )
 
         zero = jnp.zeros((CH, LANES), jnp.float32)
-        found = lax.fori_loop(0, ROWS, body, (zero,) * BLOCKS, unroll=5)
+        found = lax.fori_loop(0, ROWS, body, (zero,) * BLOCKS, unroll=UNROLL)
         for k in range(BLOCKS):
             send_buf[e, k] = found[k]
         for copy in copies(e):
@@ -381,7 +400,7 @@
             added = body(r)
             return tuple(c + t for c, t in zip(carry, added))
 
-        return lax.fori_loop(0, ROWS, step, (zero,) * sums)
+        return lax.fori_loop(0, ROWS, step, (zero,) * sums, unroll=UNROLL)
 
     def sub_copies(t):
         return [
@@ -478,7 +497,7 @@
         return (value * value * wt_ref[r],)
 
     (square,) = each_row(load_row, 1)
-    reduce_start(0, [square])
+    products = (square,)
     arrive(1)
 
     def diag_row(r):
@@ -512,7 +531,7 @@
             for r in range(ROWS):
                 y_ref[r] = y_ref[r] + y2_ref[r]
         post(exchange, y_ref)
-        reduce_middle(step)
+        reduce_start(step, products)
         arrive(exchange)
 
         def pressure_row(r, step=step, exchange=exchange):
@@ -529,6 +548,8 @@
         split_nodes(lambda r: p_ref[r])
         node_rows(plain(lhs_g), y_ref)
         post(exchange + 1, y_ref)
+        reduce_middle(step)
+        arrive(exchange + 1)
 
         sums = reduce_end(step, step + 1)
         if step == 0:
@@ -538,7 +559,6 @@
             height, squared = sums[:step], sums[step]
             length = jnp.sqrt(squared - sum(h * h for h in height))
             heights.append(height + [length])
-        arrive(exchange + 1)
 
         def direction_row(r, step=step, exchange=exchange, height=height, length=length):
             x = x_ref[r]
@@ -565,9 +585,9 @@
             return tuple(v_ref[m, r] * weighted for m in range(step + 1)) + (w * weighted,)
 
         products = each_row(image_row, step + 2)
-        reduce_start(step + 1, products)
         exchange += 3
 
+    reduce_start(KRYLOV, products)
     reduce_middle(KRYLOV)
     sums = reduce_end(KRYLOV, KRYLOV + 1)
     height, squared = sums[:KRYLOV], sums[KRYLOV]
@@ -667,21 +687,10 @@
         dma((REDUCTIONS, n_sub - 1)),
         dma((REDUCTIONS, n_slab - 1)),
         dma((REDUCTIONS, n_slab - 1)),
+        dma((INPUTS,)),
     ]
     vmem = pl.BlockSpec(memory_space=pltpu.VMEM)
-    return pl.pallas_call(
-        functools.partial(kernel, n_sub, n_slab),
-        out_shape=(
-            jax.ShapeDtypeStruct((1, 1, CASES, 4, NODES), f32),
-            jax.ShapeDtypeStruct((CASES, KRYLOV), f32),
-        ),
-        in_specs=[vmem] * 10,
-        out_specs=(vmem, vmem),
-        scratch_shapes=scratch,
-        compiler_params=pltpu.CompilerParams(
-            collective_id=0, has_side_effects=True, vmem_limit_bytes=48 * 1024 * 1024
-        ),
-    )(
+    operands = (
         adjoint_load,
         design,
         viscous_block,
@@ -693,6 +702,20 @@
         face_nodes,
         owner_ids,
     )
+    scratch += [pltpu.VMEM(x.shape, x.dtype) for x in operands]
+    return pl.pallas_call(
+        functools.partial(kernel, n_sub, n_slab),
+        out_shape=(
+            jax.ShapeDtypeStruct((1, 1, CASES, 4, NODES), f32),
+            jax.ShapeDtypeStruct((CASES, KRYLOV), f32),
+        ),
+        in_specs=[pl.BlockSpec(memory_space=pl.ANY)] * INPUTS,
+        out_specs=(vmem, vmem),
+        scratch_shapes=scratch,
+        compiler_params=pltpu.CompilerParams(
+            collective_id=0, has_side_effects=True, vmem_limit_bytes=48 * 1024 * 1024
+        ),
+    )(*operands)
 
 
 def solution(mesh):

time: 97.4 us -> 75.6 us (0.78)
  Pallas kernels: 89.4 us -> 67.6 us
    pallas_call x1, Pallas kernels: 89.4 us -> 67.6 us  [per_device(): pl.pallas_call(functools.partial(kernel, n_sub, n_slab), out_shape=(jax.S...]
where the time goes in v2:
time: 75.6 us; the launch traced here: 75.2 us
  Pallas kernels  67.6 us (89%)
  local copies, waits for them, and re-layouts  6.96 us (9%)
    pallas_call x1, Pallas kernels, per_device(): pl.pallas_call(functools.partial(kernel, n_sub, n_slab), out_shape=(jax.S...  67.6 us
    unnamed x20, local copies, waits for them, and re-layouts  6.96 us

profile of v2, /device:TPU:0, one launch (start us, length us, event | category | flops | bytes accessed | tf_op | source)
XLA Modules:
  0.0 75.2 jit_solution(18147253560578344520)
XLA Ops:
  0.6 0.0 copy-start.1
  0.6 0.7 copy.12.refs_6_
  1.3 0.0 copy-start.7
  1.3 0.7 copy.13.refs_9_
  2.0 0.0 copy-done.1
  2.0 0.0 copy-done.7
  2.0 0.0 copy-start
  2.0 0.9 %copy-done = f32[1,1,2,4,3200]{4,3,2,1,0:T(4,128)S(1)} copy-done((f32[1,1,2,4,3200]{4,3,2,1,0:T(4,128)S(1)}, f32[1,1,2,4,3200]{4,3,2,1,0:T(4,128)}, u32[]{:S(2)}) %copy-start) | copy-done | bytes 102424
  2.9 0.0 copy-start.2
  2.9 0.7 copy-done.2
  3.6 0.0 copy-start.3
  3.6 0.7 copy-done.3
  4.3 0.0 copy-start.4
  4.3 0.7 copy-done.4
  5.0 0.0 copy-start.5
  5.0 0.7 copy-done.5
  5.7 0.0 copy-start.6
  5.7 0.7 copy-done.6
  6.4 67.6 %shard_map.113 = (f32[1,1,2,4,3200]{4,3,2,1,0:T(4,128)S(1)}, f32[2,3]{1,0:T(2,128)S(1)}) custom-call(f32[1,1,2,4,3200]{4,3,2,1,0:T(4,128)S(1)} %copy-done, f32[1,1,2032]{2,1,0:T(1,128)S(1)} %copy-done.3, f32[24,24]{1,0:T(8,128)S(1)} %copy-done.1, f32[24,24]{1,0:T(8,128)S(1)} %copy-done.2, f32[8,24]{1,0:T(8,128)S(1)} %copy-done.4, f32[8,8]{1,0:T(8,128)S(1)} %copy-done.5, ...), custom_call_target="tpu_custom_call" | custom-call | tf_op jit(solution)/shard_map/pallas_call | solution.py:706
  74.0 0.6 copy.16
  74.6 0.6 copy.17
Async XLA Ops:
  0.6 1.4 %copy-start.1 = (f32[24,24]{1,0:T(8,128)S(1)}, f32[24,24]{1,0:T(8,128)}, u32[]{:S(2)}) copy-start(f32[24,24]{1,0:T(8,128)} %refs_2_.1) | copy-start | bytes 6916
  1.3 0.7 copy-start.7
  2.0 0.9 %copy-start = (f32[1,1,2,4,3200]{4,3,2,1,0:T(4,128)S(1)}, f32[1,1,2,4,3200]{4,3,2,1,0:T(4,128)}, u32[]{:S(2)}) copy-start(f32[1,1,2,4,3200]{4,3,2,1,0:T(4,128)} %refs_0_.1) | copy-start | bytes 307204
  2.9 0.7 copy-start.2
  3.6 0.7 copy-start.3
  4.3 0.7 copy-start.4
  5.0 0.7 copy-start.5
  5.7 0.7 copy-start.6

commit v3 on v2

--- a/solution.py
+++ b/solution.py
@@ -709,7 +709,7 @@
             jax.ShapeDtypeStruct((1, 1, CASES, 4, NODES), f32),
             jax.ShapeDtypeStruct((CASES, KRYLOV), f32),
         ),
-        in_specs=[pl.BlockSpec(memory_space=pl.ANY)] * INPUTS,
+        in_specs=[pl.BlockSpec(memory_space=pltpu.HBM)] * INPUTS,
         out_specs=(vmem, vmem),
         scratch_shapes=scratch,
         compiler_params=pltpu.CompilerParams(

time: 75.6 us -> 75.6 us (level)
  no operation moved by 1% of the time
where the time goes in v3:
time: 75.6 us; the launch traced here: 75.2 us
  Pallas kernels  67.6 us (89%)
  local copies, waits for them, and re-layouts  6.96 us (9%)
    pallas_call x1, Pallas kernels, per_device(): pl.pallas_call(functools.partial(kernel, n_sub, n_slab), out_shape=(jax.S...  67.6 us
    unnamed x20, local copies, waits for them, and re-layouts  6.96 us

profile of v3, /device:TPU:0, one launch (start us, length us, event | category | flops | bytes accessed | tf_op | source)
XLA Modules:
  0.0 75.2 jit_solution(18147253560578344520)
XLA Ops:
  0.6 0.0 copy-start.1
  0.6 0.7 copy.12.refs_6_
  1.3 0.0 copy-start.7
  1.3 0.7 copy.13.refs_9_
  2.0 0.0 copy-done.1
  2.0 0.0 copy-done.7
  2.0 0.0 copy-start
  2.0 0.9 %copy-done = f32[1,1,2,4,3200]{4,3,2,1,0:T(4,128)S(1)} copy-done((f32[1,1,2,4,3200]{4,3,2,1,0:T(4,128)S(1)}, f32[1,1,2,4,3200]{4,3,2,1,0:T(4,128)}, u32[]{:S(2)}) %copy-start) | copy-done | bytes 102424
  2.9 0.0 copy-start.2
  2.9 0.7 copy-done.2
  3.6 0.0 copy-start.3
  3.6 0.7 copy-done.3
  4.3 0.0 copy-start.4
  4.3 0.7 copy-done.4
  5.0 0.0 copy-start.5
  5.0 0.7 copy-done.5
  5.7 0.0 copy-start.6
  5.7 0.7 copy-done.6
  6.4 67.6 %shard_map.113 = (f32[1,1,2,4,3200]{4,3,2,1,0:T(4,128)S(1)}, f32[2,3]{1,0:T(2,128)S(1)}) custom-call(f32[1,1,2,4,3200]{4,3,2,1,0:T(4,128)S(1)} %copy-done, f32[1,1,2032]{2,1,0:T(1,128)S(1)} %copy-done.3, f32[24,24]{1,0:T(8,128)S(1)} %copy-done.1, f32[24,24]{1,0:T(8,128)S(1)} %copy-done.2, f32[8,24]{1,0:T(8,128)S(1)} %copy-done.4, f32[8,8]{1,0:T(8,128)S(1)} %copy-done.5, ...), custom_call_target="tpu_custom_call" | custom-call | tf_op jit(solution)/shard_map/pallas_call | solution.py:706
  74.0 0.6 copy.16
  74.6 0.6 copy.17
Async XLA Ops:
  0.6 1.4 %copy-start.1 = (f32[24,24]{1,0:T(8,128)S(1)}, f32[24,24]{1,0:T(8,128)}, u32[]{:S(2)}) copy-start(f32[24,24]{1,0:T(8,128)} %refs_2_.1) | copy-start | bytes 6916
  1.3 0.7 copy-start.7
  2.0 0.9 %copy-start = (f32[1,1,2,4,3200]{4,3,2,1,0:T(4,128)S(1)}, f32[1,1,2,4,3200]{4,3,2,1,0:T(4,128)}, u32[]{:S(2)}) copy-start(f32[1,1,2,4,3200]{4,3,2,1,0:T(4,128)} %refs_0_.1) | copy-start | bytes 307204
  2.9 0.7 copy-start.2
  3.6 0.7 copy-start.3
  4.3 0.7 copy-start.4
  5.0 0.7 copy-start.5
  5.7 0.7 copy-start.6
